TPU v7x, 32 devices: a whole 2x2x4 slice. The times are simulated.
32 devices in a mesh: dp: 8 (over z, y), tensor: 4 (over x, core).
Axes of the slice: x: 2, y: 2, z: 4, core: 2. Of those that a mesh axis runs over, the one named last changes fastest.
Arguments:
- inputs: bfloat16 [16384, 768], P(('dp', 'tensor')), may hold values from -6 to 6
- segments: int32 [16384], P('dp'), may hold values from 0 to 39, as said below
- w_query: bfloat16 [768, 768], P('dp', 'tensor'), may hold values from -0.21875 to 0.21875
- w_key: bfloat16 [768, 768], P('dp', 'tensor'), may hold values from -0.21875 to 0.21875
- w_value: bfloat16 [768, 768], P('dp', 'tensor'), may hold values from -0.21875 to 0.21875
- w_output: bfloat16 [768, 768], P('tensor', 'dp'), may hold values from -3.5 to 3.5
- w_hidden: bfloat16 [768, 3072], P('dp', 'tensor'), may hold values from -0.21875 to 0.21875
- w_back: bfloat16 [3072, 768], P('tensor', 'dp'), may hold values from -0.15625 to 0.15625
- gain_one: bfloat16 [768], P('dp'), may hold values from 0.5 to 1.5
- gain_two: bfloat16 [768], P('dp'), may hold values from 0.5 to 1.5
- cotangent: bfloat16 [16384, 768], P(('dp', 'tensor')), may hold values from -6 to 6
Outputs:
- result: bfloat16 [16384, 768], P(('dp', 'tensor'))
- grad_inputs: bfloat16 [16384, 768], P(('dp', 'tensor'))
- grad_query: float32 [768, 768], P('dp', 'tensor')
- grad_key: float32 [768, 768], P('dp', 'tensor')
- grad_value: float32 [768, 768], P('dp', 'tensor')
- grad_output: float32 [768, 768], P('tensor', 'dp')
- grad_hidden: float32 [768, 3072], P('dp', 'tensor')
- grad_back: float32 [3072, 768], P('tensor', 'dp')
- grad_gain_one: float32 [768], P(('dp', 'tensor'))
- grad_gain_two: float32 [768], P(('dp', 'tensor'))
Inputs may be any that keep to these rules, and one draw needn't show every extreme that they name: `segments`: segment numbers start at 0, never fall, and rise by one at each document start; every sequence of 2048 positions holds exactly five documents, the first beginning at its first position, and one of them, longer than 1536 positions, runs from before position 256 to position 1536 or past it.
All inputs are finite; a program needn't handle non-finite values.
Results may differ from a plain program's by a relative error of at most 0.018.
Values may be sent and summed in bfloat16 or wider, within the bound.
A program may use at most 128 MiB of HBM per device.

v0:
```python
import jax
import jax.numpy as jnp
from jax import lax
from jax.sharding import PartitionSpec as P

E = 64
WINDOW = 1536


def normed(value, gain):
    return value * lax.rsqrt(jnp.mean(value * value, axis=-1, keepdims=True) + 1e-05) * gain


def gelu_local(value):
    return jax.nn.gelu(value, approximate=True)


def scores_for(query_block, key_rows, segment_ids, block_start, block_rows):
    positions = jnp.arange(key_rows.shape[0], dtype=jnp.int32)
    query_pos = block_start + jnp.arange(block_rows, dtype=jnp.int32)
    query_seg = lax.dynamic_slice_in_dim(segment_ids, block_start, block_rows)
    scores = jnp.einsum(
        "qhe,khe->hqk", query_block, key_rows, preferred_element_type=jnp.float32
    ) * E ** (-0.5)
    distance = query_pos[:, None] - positions[None, :]
    allowed = (query_seg[:, None] == segment_ids[None, :]) & (distance >= 0) & (distance < WINDOW)
    return jnp.where(allowed[None], scores, -1e30)


def shards(
    inputs,
    segments,
    w_query,
    w_key,
    w_value,
    w_output,
    w_hidden,
    w_back,
    gain_one,
    gain_two,
    cotangent,
):
    owned = (w_query, w_key, w_value, w_output, w_hidden, w_back, gain_one, gain_two)
    gathered = (
        lax.all_gather(owned[0], "dp", axis=0, tiled=True),
        lax.all_gather(owned[1], "dp", axis=0, tiled=True),
        lax.all_gather(owned[2], "dp", axis=0, tiled=True),
        lax.all_gather(owned[3], "dp", axis=1, tiled=True),
        lax.all_gather(owned[4], "dp", axis=0, tiled=True),
        lax.all_gather(owned[5], "dp", axis=1, tiled=True),
        lax.all_gather(owned[6], "dp", axis=0, tiled=True),
        lax.all_gather(owned[7], "dp", axis=0, tiled=True),
    )
    total_rows = segments.shape[0]
    block_rows = min(512, total_rows)
    blocks = total_rows // block_rows
    width = gathered[0].shape[1]
    heads_here = width // E
    scale = E ** (-0.5)
    starts = jnp.arange(blocks, dtype=jnp.int32) * block_rows
    w_joined = jnp.concatenate([gathered[0], gathered[1], gathered[2]], axis=1)
    gain_first = gathered[6].astype(jnp.float32)
    gain_second = gathered[7].astype(jnp.float32)
    inputs_f = inputs.astype(jnp.float32)
    normed_one = normed(inputs_f, gain_first).astype(jnp.bfloat16)
    full_one = lax.all_gather(normed_one, "tensor", axis=0, tiled=True)
    joined = jnp.dot(full_one, w_joined, preferred_element_type=jnp.float32).astype(jnp.bfloat16)
    query_rows = joined[:, :width].reshape(total_rows, heads_here, E)
    key_rows = joined[:, width : 2 * width].reshape(total_rows, heads_here, E)
    value_rows = joined[:, 2 * width :].reshape(total_rows, heads_here, E)
    query_blocks = query_rows.reshape(blocks, block_rows, heads_here, E)

    def forward_block(packed):
        query_block, block_start = packed
        scores = scores_for(query_block, key_rows, segments, block_start, block_rows)
        row_top = jnp.max(scores, axis=-1, keepdims=True)
        weights_exp = jnp.exp(scores - row_top)
        totals = jnp.sum(weights_exp, axis=-1, keepdims=True)
        probability = (weights_exp / totals).astype(jnp.bfloat16)
        attended_block = jnp.einsum(
            "hqk,khe->qhe", probability, value_rows, preferred_element_type=jnp.float32
        )
        return (attended_block.astype(jnp.bfloat16), (row_top + jnp.log(totals))[..., 0])

    attended, log_sums = lax.map(forward_block, (query_blocks, starts))
    attended = attended.reshape(total_rows, width)
    w_out_full = gathered[3]
    own_attended = lax.all_to_all(attended, "tensor", split_axis=0, concat_axis=1, tiled=True)
    w_out_all = lax.all_gather(w_out_full, "tensor", axis=0, tiled=True)
    attn_branch = jnp.dot(own_attended, w_out_all, preferred_element_type=jnp.float32)
    middle = inputs_f + attn_branch
    normed_two = normed(middle, gain_second).astype(jnp.bfloat16)
    full_two = lax.all_gather(normed_two, "tensor", axis=0, tiled=True)
    hidden = jnp.dot(full_two, gathered[4], preferred_element_type=jnp.float32)
    active = gelu_local(hidden).astype(jnp.bfloat16)
    w_back_full = gathered[5]
    result = middle + lax.psum_scatter(
        jnp.dot(active, w_back_full, preferred_element_type=jnp.float32).astype(jnp.bfloat16),
        "tensor",
        scatter_dimension=0,
        tiled=True,
    ).astype(jnp.float32)
    gathered = (
        lax.all_gather(owned[0], "dp", axis=0, tiled=True),
        lax.all_gather(owned[1], "dp", axis=0, tiled=True),
        lax.all_gather(owned[2], "dp", axis=0, tiled=True),
        lax.all_gather(owned[3], "dp", axis=1, tiled=True),
        lax.all_gather(owned[4], "dp", axis=0, tiled=True),
        lax.all_gather(owned[5], "dp", axis=1, tiled=True),
        lax.all_gather(owned[6], "dp", axis=0, tiled=True),
        lax.all_gather(owned[7], "dp", axis=0, tiled=True),
    )
    w_joined = jnp.concatenate([gathered[0], gathered[1], gathered[2]], axis=1)
    grad_out = cotangent.astype(jnp.float32)
    full_grad = lax.all_gather(cotangent, "tensor", axis=0, tiled=True)
    grad_w_back = jnp.einsum("rf,rd->fd", active, full_grad, preferred_element_type=jnp.float32)
    grad_active = jnp.einsum(
        "rd,fd->rf", full_grad, gathered[5], preferred_element_type=jnp.float32
    )
    gelu_pull = jax.vjp(gelu_local, hidden)[1]
    grad_hidden_rows = gelu_pull(grad_active)[0].astype(jnp.bfloat16)
    grad_w_hidden = jnp.einsum(
        "rd,rf->df", full_two, grad_hidden_rows, preferred_element_type=jnp.float32
    )
    w_hidden_full = gathered[4]
    piece = grad_hidden_rows
    grad_normed_two = lax.psum_scatter(
        jnp.einsum("rf,df->rd", piece, w_hidden_full, preferred_element_type=jnp.float32).astype(
            jnp.bfloat16
        ),
        "tensor",
        scatter_dimension=0,
        tiled=True,
    ).astype(jnp.float32)
    second_pull = jax.vjp(normed, middle, gain_second)[1]
    grad_mid_norm, grad_second = second_pull(grad_normed_two)
    grad_middle = grad_out + grad_mid_norm
    full_middle = lax.all_gather(grad_middle.astype(jnp.bfloat16), "tensor", axis=0, tiled=True)
    grad_w_output = jnp.einsum(
        "rh,rd->hd", attended, full_middle, preferred_element_type=jnp.float32
    )
    grad_attended = jnp.einsum(
        "rd,hd->rh", full_middle, gathered[3], preferred_element_type=jnp.float32
    ).astype(jnp.bfloat16)

    def backward_block(carry, packed):
        grad_keys, grad_values = carry
        query_block, grad_block, log_block, block_start = packed
        scores = scores_for(query_block, key_rows, segments, block_start, block_rows)
        probability = jnp.exp(scores - log_block[..., None])
        grad_values = grad_values + jnp.einsum(
            "hqk,qhe->khe",
            probability.astype(jnp.bfloat16),
            grad_block,
            preferred_element_type=jnp.float32,
        )
        grad_probs = jnp.einsum(
            "qhe,khe->hqk", grad_block, value_rows, preferred_element_type=jnp.float32
        )
        delta_rows = jnp.sum(grad_probs * probability, axis=-1, keepdims=True)
        grad_scores = (probability * (grad_probs - delta_rows)).astype(jnp.bfloat16)
        grad_query_block = (
            jnp.einsum("hqk,khe->qhe", grad_scores, key_rows, preferred_element_type=jnp.float32)
            * scale
        )
        grad_keys = (
            grad_keys
            + jnp.einsum(
                "hqk,qhe->khe", grad_scores, query_block, preferred_element_type=jnp.float32
            )
            * scale
        )
        return ((grad_keys, grad_values), grad_query_block)

    zero_state = jnp.zeros((total_rows, heads_here, E), jnp.float32)
    grad_blocks = grad_attended.reshape(blocks, block_rows, heads_here, E)
    (grad_keys, grad_values), grad_queries = lax.scan(
        backward_block, (zero_state, zero_state), (query_blocks, grad_blocks, log_sums, starts)
    )
    grad_joined = jnp.concatenate(
        [
            grad_queries.reshape(total_rows, width),
            grad_keys.reshape(total_rows, width),
            grad_values.reshape(total_rows, width),
        ],
        axis=1,
    ).astype(jnp.bfloat16)
    grad_w_joined = jnp.einsum(
        "rd,rc->dc", full_one, grad_joined, preferred_element_type=jnp.float32
    )
    piece = grad_joined
    grad_normed_one = lax.psum_scatter(
        jnp.einsum("rc,dc->rd", piece, w_joined, preferred_element_type=jnp.float32).astype(
            jnp.bfloat16
        ),
        "tensor",
        scatter_dimension=0,
        tiled=True,
    ).astype(jnp.float32)
    first_pull = jax.vjp(normed, inputs_f, gain_first)[1]
    grad_in_norm, grad_first = first_pull(grad_normed_one)
    grad_inputs = grad_middle + grad_in_norm
    weight_sums = (
        lax.psum_scatter(grad_w_joined[:, :width], "dp", scatter_dimension=0, tiled=True),
        lax.psum_scatter(
            grad_w_joined[:, width : 2 * width], "dp", scatter_dimension=0, tiled=True
        ),
        lax.psum_scatter(grad_w_joined[:, 2 * width :], "dp", scatter_dimension=0, tiled=True),
        lax.psum_scatter(grad_w_output, "dp", scatter_dimension=1, tiled=True),
        lax.psum_scatter(grad_w_hidden, "dp", scatter_dimension=0, tiled=True),
        lax.psum_scatter(grad_w_back, "dp", scatter_dimension=1, tiled=True),
    )
    gain_sums = (
        lax.psum_scatter(grad_first, ("dp", "tensor"), scatter_dimension=0, tiled=True),
        lax.psum_scatter(grad_second, ("dp", "tensor"), scatter_dimension=0, tiled=True),
    )
    return (
        result.astype(jnp.bfloat16),
        grad_inputs.astype(jnp.bfloat16),
        weight_sums[0],
        weight_sums[1],
        weight_sums[2],
        weight_sums[3],
        weight_sums[4],
        weight_sums[5],
        gain_sums[0],
        gain_sums[1],
    )


def solution(mesh):
    in_specs = (
        P(("dp", "tensor"), None),
        P("dp"),
        P("dp", "tensor"),
        P("dp", "tensor"),
        P("dp", "tensor"),
        P("tensor", "dp"),
        P("dp", "tensor"),
        P("tensor", "dp"),
        P("dp"),
        P("dp"),
        P(("dp", "tensor"), None),
    )
    out_specs = (
        P(("dp", "tensor"), None),
        P(("dp", "tensor"), None),
        P("dp", "tensor"),
        P("dp", "tensor"),
        P("dp", "tensor"),
        P("tensor", "dp"),
        P("dp", "tensor"),
        P("tensor", "dp"),
        P(("dp", "tensor")),
        P(("dp", "tensor")),
    )
    return jax.shard_map(shards, mesh=mesh, in_specs=in_specs, out_specs=out_specs, check_vma=False)
```

profile of v0, /device:TPU:0, one launch (start us, length us, event | category | flops | bytes accessed | tf_op | source)
XLA Modules:
  0.0 1014.2 jit_solution(13211570394139215744)
XLA Ops:
  12.3 23.1 %all-reduce.5 = (bf16[768]{0:T(1024)(128)(2,1)S(1)}, bf16[768]{0:T(1024)(128)(2,1)S(1)}) all-reduce(bf16[768]{0:T(1024)(128)(2,1)S(1)} %dynamic-update-slice, bf16[768]{0:T(1024)(128)(2,1)S(1)} %dynamic-update-slice.1), channel_id=1, replica_groups=mesh['dp'=8,'tensor'=4] {'dp'}, use_global_device_ids=true, to_apply=%add | all-reduce | flops 1536 | bytes 6144
  38.4 31.0 %all_gather.50 = bf16[192,768]{0,1:T(8,128)(2,1)S(1)} all-gather(bf16[192,96]{0,1:T(8,128)(2,1)S(1)} %copy.45), channel_id=1, replica_groups=mesh['dp'=8,'tensor'=4] {'dp'}, dimensions={1}, use_global_device_ids=true | all-gather | bytes 331776 | tf_op jit(solution)/shard_map/all_gather | solution.py:48
  72.3 31.2 %all_gather.47 = bf16[768,192]{1,0:T(8,128)(2,1)S(1)} all-gather(bf16[96,192]{1,0:T(8,128)(2,1)S(1)} %copy-done.30), channel_id=1, replica_groups=mesh['dp'=8,'tensor'=4] {'dp'}, dimensions={0}, use_global_device_ids=true | all-gather | bytes 331776 | tf_op jit(solution)/shard_map/all_gather | solution.py:45
  103.6 31.9 %all_gather.48 = bf16[768,192]{1,0:T(8,128)(2,1)S(1)} all-gather(bf16[96,192]{1,0:T(8,128)(2,1)S(1)} %copy-done.31), channel_id=1, replica_groups=mesh['dp'=8,'tensor'=4] {'dp'}, dimensions={0}, use_global_device_ids=true | all-gather | bytes 331776 | tf_op jit(solution)/shard_map/all_gather | solution.py:46
  135.5 31.0 %all_gather.49 = bf16[768,192]{1,0:T(8,128)(2,1)S(1)} all-gather(bf16[96,192]{1,0:T(8,128)(2,1)S(1)} %copy-done.32), channel_id=1, replica_groups=mesh['dp'=8,'tensor'=4] {'dp'}, dimensions={0}, use_global_device_ids=true | all-gather | bytes 331776 | tf_op jit(solution)/shard_map/all_gather | solution.py:47
  167.2 4.1 convolution_convert_fusion.3
  172.2 105.1 %while.27 = (s32[]{:T(128)}, bf16[4,512,3,64]{1,3,2,0:T(8,128)(2,1)}, f32[4,3,512]{2,1,0:T(4,128)}, s32[4]{0:T(128)S(1)}, s32[2048]{0:T(1024)S(1)}, /*index=5*/b...) while((s32[]{:T(128)}, ...), condition=%wide.region_4.5_spmd, body=%wide.region_1.4_spmd.sunk | while | flops 849443840 | bytes 43978932 | solution.py:85
  177.8 6.0 fusion.130
  183.8 6.9 fusion.131
  190.7 7.3 fusion.132
  204.1 6.0 fusion.130
  210.1 6.8 fusion.131
  216.9 7.3 fusion.132
  230.4 6.0 fusion.130
  236.4 6.8 fusion.131
  243.1 7.3 fusion.132
  256.6 6.0 fusion.130
  262.6 6.8 fusion.131
  269.3 7.3 fusion.132
  277.3 3.5 all-to-all-start
  281.1 11.3 %all-to-all-done = bf16[4,512,192]{1,2,0:T(8,128)(2,1)S(1)} async-done(((bf16[4,512,192]{1,2,0:T(8,128)(2,1)}), bf16[4,512,192]{1,2,0:T(8,128)(2,1)S(1)}, u32[]{:S(2)}, u32[]{:S(2)}) %all-to-all-start) | async-done | bytes 786464 | tf_op jit(solution)/shard_map/all_to_all | solution.py:88
  297.4 7.5 fusion.80
  304.9 17.4 %all-gather.12.cloned.1.call-done = bf16[2048,768]{1,0:T(8,128)(2,1)} async-done(((bf16[512,768]{1,0:T(8,128)(2,1)}), bf16[2048,768]{1,0:T(8,128)(2,1)}) %all-gather.12.cloned.1.call-update) | async-done | bytes 3145744 | tf_op jit(solution)/shard_map/all_gather | solution.py:93
  322.3 11.2 %fusion.56 = (bf16[2048,768]{1,0:T(8,128)(2,1)S(1)}, f32[2048,768]{1,0:T(8,128)}) fusion(f32[2048,768]{1,0:T(8,128)} %fusion.80, bf16[2048,768]{1,0:T(8,128)(2,1)} %all-gather.12.cloned.1.call-done, bf16[768,768]{1,0:T(8,128)(2,1)} %all-gather.14.cloned.1.call-done), kind=kOutput, calls=%fused_computation.67 | convolution fusion | flops 2447376384 | bytes 20054016 | tf_op jit(solution)/shard_map/dot_general | solution.py:94
  335.2 4.0 convolution_convert_fusion.1
  339.3 38.1 %reduce-scatter.20.cloned.1.call-done = bf16[512,768]{1,0:T(8,128)(2,1)} async-done(((bf16[2048,768]{1,0:T(8,128)(2,1)}), bf16[512,768]{1,0:T(8,128)(2,1)}) %reduce-scatter.20.cloned.1.call-update) | async-done | bytes 786448 | tf_op jit(solution)/shard_map/reduce_scatter | solution.py:127
  386.0 25.8 %all-gather.20.cloned.1.call-done = bf16[2048,768]{1,0:T(8,128)(2,1)} async-done(((bf16[512,768]{1,0:T(8,128)(2,1)}), bf16[2048,768]{1,0:T(8,128)(2,1)}) %all-gather.20.cloned.1.call-update) | async-done | bytes 3145744 | tf_op jit(solution)/shard_map/all_gather | solution.py:138
  411.8 3.1 convolution_convert_fusion.4
  415.7 4.4 convolution_bitcast_fusion
  420.1 157.9 %while.28 = (s32[]{:T(128)}, f32[2048,3,64]{0,2,1:T(8,128)}, f32[2048,3,64]{0,2,1:T(8,128)}, bf16[4,512,3,64]{1,3,2,0:T(8,128)(2,1)}, bf16[4,512,3,64]{1,3,2,0:T...) while((s32[]{:T(128)}, f32[2048,3,64]{0,2,1:T(8,128)}, ...), condition=%wide.region_11.12_spmd.clone, body=%wide.region_9.11_spmd.clone.sunk | while | flops 2068806656 | bytes 156695008 | solution.py:177
  436.5 3.0 fusion.142
  439.6 4.7 fusion.145
  444.3 5.8 multiply_reduce_fusion.3
  450.1 6.1 multiply_convert_fusion.6
  456.2 5.8 fusion.146
  462.0 3.5 fusion.144
  472.0 3.0 fusion.142
  475.1 6.1 fusion.145
  481.2 5.8 multiply_reduce_fusion.3
  487.0 6.1 multiply_convert_fusion.6
  493.1 5.8 fusion.146
  498.9 4.1 fusion.144
  512.5 6.1 fusion.145
  518.6 5.8 multiply_reduce_fusion.3
  524.4 6.1 multiply_convert_fusion.6
  530.5 5.8 fusion.146
  536.3 4.1 fusion.144
  549.9 6.1 fusion.145
  556.0 5.8 multiply_reduce_fusion.3
  561.8 6.1 multiply_convert_fusion.6
  567.9 5.8 fusion.146
  573.7 4.1 fusion.144
  581.9 4.6 convolution_convert_fusion
  587.7 8.3 convolution_convert_fusion.2
  596.1 7.1 fusion.81
  603.5 8.8 fusion.77
  612.4 3.9 fusion.70
  627.0 39.9 %all-reduce.4 = (f32[768]{0:T(1024)S(1)}, f32[768]{0:T(1024)S(1)}) all-reduce(f32[768]{0:T(1024)S(1)} %get-tuple-element.271, f32[768]{0:T(1024)S(1)} %copy-done.40), channel_id=11, replica_groups=mesh['dp'=8,'tensor'=4] {'dp','tensor'}, use_global_device_ids=true, to_apply=%region_21.22.clone | all-reduce | flops 1536 | bytes 12288
  668.1 3.7 fusion.67
  671.8 67.0 %reduce-scatter.24.cloned.1.call-done = f32[96,768]{1,0:T(8,128)} async-done(((f32[768,768]{1,0:T(8,128)}), f32[96,768]{1,0:T(8,128)}) %reduce-scatter.24.cloned.1.call-update) | async-done | bytes 294928 | tf_op jit(solution)/shard_map/reduce_scatter | solution.py:210
  738.8 72.3 %reduce-scatter.26.cloned.1.call-done = f32[768,96]{0,1:T(8,128)} async-done(((f32[768,768]{0,1:T(8,128)}), f32[768,96]{0,1:T(8,128)}) %reduce-scatter.26.cloned.1.call-update) | async-done | bytes 294928 | tf_op jit(solution)/shard_map/reduce_scatter | solution.py:211
  811.1 65.3 %reduce-scatter.32.cloned.1.call-done = f32[96,192]{1,0:T(8,128)} async-done(((f32[768,192]{1,0:T(8,128)}), f32[96,192]{1,0:T(8,128)}) %reduce-scatter.32.cloned.1.call-update) | async-done | bytes 73744
  876.4 65.6 %reduce-scatter.30.cloned.1.call-done = f32[96,192]{1,0:T(8,128)} async-done(((f32[768,192]{1,0:T(8,128)}), f32[96,192]{1,0:T(8,128)}) %reduce-scatter.30.cloned.1.call-update) | async-done | bytes 73744
  942.0 65.2 %reduce-scatter.28.cloned.1.call-done = f32[96,192]{1,0:T(8,128)} async-done(((f32[768,192]{1,0:T(8,128)}), f32[96,192]{1,0:T(8,128)}) %reduce-scatter.28.cloned.1.call-update) | async-done | bytes 73744
  (266 shorter events, 85.9 us)
Async XLA Ops:
  7.2 31.1 %copy-start.33 = (bf16[192,96]{1,0:T(8,128)(2,1)S(1)}, bf16[192,96]{1,0:T(8,128)(2,1)}, u32[]{:S(2)}) copy-start(bf16[192,96]{1,0:T(8,128)(2,1)} %param.20) | copy-start | bytes 110596
  7.2 65.1 %copy-start.30 = (bf16[96,192]{1,0:T(8,128)(2,1)S(1)}, bf16[96,192]{1,0:T(8,128)(2,1)}, u32[]{:S(2)}) copy-start(bf16[96,192]{1,0:T(8,128)(2,1)} %param.17) | copy-start | bytes 110596
  7.2 96.4 %copy-start.31 = (bf16[96,192]{1,0:T(8,128)(2,1)S(1)}, bf16[96,192]{1,0:T(8,128)(2,1)}, u32[]{:S(2)}) copy-start(bf16[96,192]{1,0:T(8,128)(2,1)} %param.18) | copy-start | bytes 110596
  7.2 159.2 %all-gather.8.cloned.1.call-start = ((), (), s32[]{:S(2)}) async-start(), calls=%async_computation.10 | async-start | bytes 3932160 | tf_op jit(solution)/shard_map/all_gather | solution.py:66
  8.6 63.7 %copy-start.38 = (f32[512]{0:T(512)}, f32[512]{0:T(512)S(1)}, u32[]{:S(2)}) copy-start(f32[512]{0:T(512)S(1)} %fusion.68) | copy-start | bytes 6148
  8.6 126.9 %copy-start.32 = (bf16[96,192]{1,0:T(8,128)(2,1)S(1)}, bf16[96,192]{1,0:T(8,128)(2,1)}, u32[]{:S(2)}) copy-start(bf16[96,192]{1,0:T(8,128)(2,1)} %param.19) | copy-start | bytes 110596
  8.7 63.7 %copy-start.34 = (f32[512]{0:T(512)}, f32[512]{0:T(512)S(1)}, u32[]{:S(2)}) copy-start(f32[512]{0:T(512)S(1)} %fusion.71) | copy-start | bytes 6148
  38.3 242.9 %all-gather.10.cloned.1.call-start = ((), (), s32[]{:S(2)}) async-start(), calls=%async_computation.11 | async-start | bytes 1474560 | tf_op jit(solution)/shard_map/all_gather | solution.py:89
  69.5 97.0 %copy-start.14 = (bf16[192,768]{0,1:T(8,128)(2,1)}, bf16[192,768]{0,1:T(8,128)(2,1)S(1)}, u32[]{:S(2)}) copy-start(bf16[192,768]{0,1:T(8,128)(2,1)S(1)} %all_gather.50) | copy-start | bytes 884740
  70.4 227.0 %all-gather.16.cloned.1.call-start = ((), (), s32[]{:S(2)}) async-start(), calls=%async_computation.14 | async-start | bytes 1327104 | tf_op jit(solution)/shard_map/all_gather | solution.py:50
  71.1 226.3 %all-gather.18.cloned.1.call-start = ((), (), s32[]{:S(2)}) async-start(), calls=%async_computation.16 | async-start | bytes 3932160 | tf_op jit(solution)/shard_map/all_gather | solution.py:115
  71.7 233.2 %all-gather.14.cloned.1.call-start = ((), (), s32[]{:S(2)}) async-start(), calls=%async_computation.13 | async-start | bytes 1327104 | tf_op jit(solution)/shard_map/all_gather | solution.py:49
  103.6 62.9 %copy-start.18 = (bf16[768,192]{1,0:T(8,128)(2,1)}, bf16[768,192]{1,0:T(8,128)(2,1)S(1)}, u32[]{:S(2)}) copy-start(bf16[768,192]{1,0:T(8,128)(2,1)S(1)} %all_gather.47) | copy-start | bytes 884740
  135.5 31.0 %copy-start.20 = (bf16[768,192]{1,0:T(8,128)(2,1)}, bf16[768,192]{1,0:T(8,128)(2,1)S(1)}, u32[]{:S(2)}) copy-start(bf16[768,192]{1,0:T(8,128)(2,1)S(1)} %all_gather.48) | copy-start | bytes 884740
  277.3 15.1 %copy-start.10 = (bf16[4,512,3,64]{1,3,2,0:T(8,128)(2,1)}, bf16[4,512,3,64]{1,3,2,0:T(8,128)(2,1)S(1)}, u32[]{:S(2)}) copy-start(bf16[4,512,3,64]{1,3,2,0:T(8,128)(2,1)S(1)} %get-tuple-element.548) | copy-start | bytes 2359300
  277.3 15.1 %copy-start.43 = (s32[4]{0:T(128)}, s32[4]{0:T(128)S(1)}, u32[]{:S(2)}) copy-start(s32[4]{0:T(128)S(1)} %get-tuple-element.599) | copy-start | bytes 52
  277.3 15.1 %all-to-all-start = ((bf16[4,512,192]{1,2,0:T(8,128)(2,1)}), bf16[4,512,192]{1,2,0:T(8,128)(2,1)S(1)}, u32[]{:S(2)}, u32[]{:S(2)}) async-start(bf16[4,512,192]{1,2,0:T(8,128)(2,1)} %bitcast.8), calls=%async_computation | async-start | bytes 1572864 | tf_op jit(solution)/shard_map/all_to_all | solution.py:88
  280.8 41.5 %all-gather.12.cloned.1.call-start = ((), (), s32[]{:S(2)}) async-start(), calls=%async_computation.12 | async-start | bytes 3932160 | tf_op jit(solution)/shard_map/all_gather | solution.py:93
  281.1 98.6 %copy-start.24 = (f32[768]{0:T(1024)}, f32[768]{0:T(1024)S(1)}, u32[]{:S(2)}) copy-start(f32[768]{0:T(1024)S(1)} %convert_element_type.77) | copy-start | bytes 9220
  295.9 83.8 %copy-start.7 = (f32[512,768]{1,0:T(8,128)}, f32[512,768]{1,0:T(8,128)S(1)}, u32[]{:S(2)}) copy-start(f32[512,768]{1,0:T(8,128)S(1)} %get-tuple-element.328) | copy-start | bytes 4718596
  295.9 83.8 %copy-start.28 = (f32[512]{0:T(512)}, f32[512]{0:T(512)S(1)}, u32[]{:S(2)}) copy-start(f32[512]{0:T(512)S(1)} %fusion.72) | copy-start | bytes 6148
  297.3 80.1 %reduce-scatter.20.cloned.1.call-start = ((), (), s32[]{:S(2)}) async-start(), calls=%async_computation.17 | async-start | bytes 3932160 | tf_op jit(solution)/shard_map/reduce_scatter | solution.py:127
  322.3 12.9 %copy-start.42 = (bf16[768,768]{1,0:T(8,128)(2,1)S(1)}, bf16[768,768]{1,0:T(8,128)(2,1)}, u32[]{:S(2)}) copy-start(bf16[768,768]{1,0:T(8,128)(2,1)} %all-gather.14.cloned.1.call-done) | copy-start | bytes 3538948
  339.2 72.6 %all-gather.20.cloned.1.call-start = ((), (), s32[]{:S(2)}) async-start(), calls=%async_computation.18 | async-start | bytes 3932160 | tf_op jit(solution)/shard_map/all_gather | solution.py:138
  380.3 31.5 %copy-start.15 = (bf16[192,768]{0,1:T(8,128)(2,1)S(1)}, bf16[192,768]{0,1:T(8,128)(2,1)}, u32[]{:S(2)}) copy-start(bf16[192,768]{0,1:T(8,128)(2,1)} %copy-done.14) | copy-start | bytes 884740
  383.1 240.3 %reduce-scatter.34.cloned.1.call-start = ((), (), s32[]{:S(2)}) async-start(), calls=%async_computation.25 | async-start | bytes 884736
  415.7 4.5 copy-start.44
  420.1 205.0 %reduce-scatter.22.cloned.1.call-start = ((), (), s32[]{:S(2)}) async-start(), calls=%async_computation.19 | async-start | bytes 3932160 | tf_op jit(solution)/shard_map/reduce_scatter | solution.py:192
  430.1 9.4 copy-start.2
  430.1 9.4 copy-start.5
  430.1 9.4 copy-start.12
  456.2 5.9 copy-start
  465.6 9.4 copy-start.2
  465.6 9.4 copy-start.5
  465.6 9.4 copy-start.12
  493.1 5.8 copy-start
  498.9 4.1 copy-start.6
  498.9 4.1 copy-start.13
  503.0 9.4 copy-start.2
  503.0 9.4 copy-start.5
  503.1 9.4 copy-start.12
  530.5 5.8 copy-start
  536.3 4.1 copy-start.13
  540.4 9.4 copy-start.2
  540.5 9.4 copy-start.5
  540.5 9.4 copy-start.12
  567.9 5.8 copy-start
  573.7 4.1 copy-start.13
  586.5 81.6 %reduce-scatter.18.cloned.1.call-start = ((), (), s32[]{:S(2)}) async-start(), calls=%async_computation.15 | async-start | bytes 3932160 | tf_op jit(solution)/shard_map/reduce_scatter | solution.py:97
  596.0 142.8 %reduce-scatter.24.cloned.1.call-start = ((), (), s32[]{:S(2)}) async-start(), calls=%async_computation.20 | async-start | bytes 2654208 | tf_op jit(solution)/shard_map/reduce_scatter | solution.py:210
  603.2 207.9 %reduce-scatter.26.cloned.1.call-start = ((), (), s32[]{:S(2)}) async-start(), calls=%async_computation.21 | async-start | bytes 2654208 | tf_op jit(solution)/shard_map/reduce_scatter | solution.py:211
  612.3 264.1 %reduce-scatter.32.cloned.1.call-start = ((), (), s32[]{:S(2)}) async-start(), calls=%async_computation.24 | async-start | bytes 884736
  617.4 7.7 copy-start.9
  617.4 7.7 copy-start.27
  617.4 7.7 copy-start.35
  618.6 8.4 copy-start.40
  618.6 49.5 %copy-start.39 = (f32[512]{0:T(512)S(1)}, f32[512]{0:T(512)}, u32[]{:S(2)}) copy-start(f32[512]{0:T(512)} %copy-done.38) | copy-start | bytes 6148
  618.6 49.5 %copy-start.8 = (f32[512,768]{1,0:T(8,128)S(1)}, f32[512,768]{1,0:T(8,128)}, u32[]{:S(2)}) copy-start(f32[512,768]{1,0:T(8,128)} %copy-done.7) | copy-start | bytes 4718596
  618.6 49.5 %copy-start.11 = (bf16[512,768]{1,0:T(8,128)(2,1)S(1)}, bf16[512,768]{1,0:T(8,128)(2,1)}, u32[]{:S(2)}) copy-start(bf16[512,768]{1,0:T(8,128)(2,1)} %param.25) | copy-start | bytes 2359300
  618.6 49.5 %copy-start.25 = (f32[768]{0:T(1024)S(1)}, f32[768]{0:T(1024)}, u32[]{:S(2)}) copy-start(f32[768]{0:T(1024)} %copy-done.24) | copy-start | bytes 9220
  618.6 49.5 %copy-start.29 = (f32[512]{0:T(512)S(1)}, f32[512]{0:T(512)}, u32[]{:S(2)}) copy-start(f32[512]{0:T(512)} %copy-done.28) | copy-start | bytes 6148
  618.6 49.5 %copy-start.37 = (f32[512]{0:T(512)S(1)}, f32[512]{0:T(512)}, u32[]{:S(2)}) copy-start(f32[512]{0:T(512)} %copy-done.36) | copy-start | bytes 6148
  618.6 323.3 %reduce-scatter.30.cloned.1.call-start = ((), (), s32[]{:S(2)}) async-start(), calls=%async_computation.23 | async-start | bytes 884736
  621.1 386.1 %reduce-scatter.28.cloned.1.call-start = ((), (), s32[]{:S(2)}) async-start(), calls=%async_computation.22 | async-start | bytes 884736
  (23 other events, 57.8 us)
Sparse Core Ops, SparseCore 0:
  38.4 25.7 all-gather.7
  70.5 14.7 all-gather.9
  87.4 44.1 all-gather.15
  133.0 28.0 all-gather.17
  163.2 41.0 all-gather.13
  297.4 24.8 all-gather.11
  339.4 37.9 reduce-scatter.19
  383.3 28.5 all-gather.19
  420.2 62.4 reduce-scatter.33
  586.6 37.9 reduce-scatter.21
  627.3 38.1 reduce-scatter.17
  669.4 69.3 reduce-scatter.23
  742.8 68.2 reduce-scatter.25
  814.8 61.5 reduce-scatter.31
  880.5 61.4 reduce-scatter.29
  945.7 61.4 reduce-scatter.27
where the time goes:
time: 1020 us; the launch traced here: 1010 us
  waiting for transfers between devices  430 us (42%)
  matrix products  220 us (22%)
  blocking collectives  188 us (18%)
  other arithmetic  94.8 us (9%)
  local copies, waits for them, and re-layouts  34.6 us (3%)
  loops' own time  26.4 us (3%)
  between operations  15.7 us (2%)
    unnamed x20, waiting for transfers between devices  198 us
    reduce_scatter x1, waiting for transfers between devices, shards(): lax.psum_scatter(grad_w_back, 'dp', scatter_dimension=1, tiled=True)  72.3 us
    reduce_scatter x1, waiting for transfers between devices, shards(): lax.psum_scatter(grad_w_hidden, 'dp', scatter_dimension=0, tiled=True)  67 us
    unnamed x2, blocking collectives  63 us
    reduce_scatter x1, waiting for transfers between devices, shards(): lax.psum_scatter(jnp.einsum('rf,df->rd', piece, w_hidden_full, preferred_...  38.1 us
    dot_general x8, matrix products, scores_for(): jnp.einsum('qhe,khe->hqk', query_block, key_rows, preferred_element_type=...  35.9 us
    all_gather x1, blocking collectives, shards(): lax.all_gather(owned[1], 'dp', axis=0, tiled=True)  31.9 us
    all_gather x1, blocking collectives, shards(): lax.all_gather(owned[0], 'dp', axis=0, tiled=True)  31.2 us
  transfers between devices with their start and end apart: 17, of which 9 were waited for; matrix products, arithmetic and copies ran while one was open for 30% of the time, Pallas kernels for 0%

commit v1 on v0

--- a/solution.py
+++ b/solution.py
@@ -1,10 +1,797 @@
+import functools
+
 import jax
 import jax.numpy as jnp
 from jax import lax
+from jax.experimental import pallas as pl
+from jax.experimental.pallas import tpu as pltpu
 from jax.sharding import PartitionSpec as P
 
+MESH = pl.DeviceIdType.MESH
+f32, bf = jnp.float32, jnp.bfloat16
 E = 64
 WINDOW = 1536
+B = 256
+LOG2E = 1.4426950408889634
+SCALE = E**-0.5
+FILL = -1e30
+CUT = 1280
+NZ = 4
+
+
+def nn(a, b):
+    return lax.dot_general(a, b, (((1,), (0,)), ((), ())), preferred_element_type=f32)
+
+
+def nt(a, b):
+    return lax.dot_general(a, b, (((1,), (1,)), ((), ())), preferred_element_type=f32)
+
+
+def tn(a, b):
+    return lax.dot_general(a, b, (((0,), (0,)), ((), ())), preferred_element_type=f32)
+
+
+class Place:
+    def __init__(self):
+        self.dp = lax.axis_index("dp")
+        self.t = lax.axis_index("tensor")
+        self.z, self.y = lax.div(self.dp, 2), lax.rem(self.dp, 2)
+        self.x, self.c = lax.div(self.t, 2), lax.rem(self.t, 2)
+
+    def at(self, z=None, y=None, x=None, c=None):
+        z = self.z if z is None else z
+        y = self.y if y is None else y
+        x = self.x if x is None else x
+        c = self.c if c is None else c
+        return (z * 2 + y, x * 2 + c)
+
+    def greet(self, far_z):
+        barrier = pltpu.get_barrier_semaphore()
+        x, y, z, c = self.x, self.y, self.z, self.c
+        near = [self.at(y=1 - y), self.at(x=1 - x), self.at(c=1 - c), self.at(x=1 - x, c=1 - c)]
+        for there in near:
+            pl.semaphore_signal(barrier, inc=1, device_id=there, device_id_type=MESH)
+        for step in range(1, NZ):
+            pl.semaphore_signal(
+                barrier, inc=1, device_id=self.at(z=lax.rem(z + step, NZ)), device_id_type=MESH
+            )
+        pl.semaphore_wait(barrier, len(near) + NZ - 1)
+
+
+class Lanes:
+    def __init__(self, send, recv):
+        self.send, self.recv, self.n, self.base, self.late = send, recv, 0, {}, []
+
+    def block(self, name, count):
+        self.base[name] = self.n
+        self.n += count
+
+    def copy(self, name, k, src, dst, there):
+        i = self.base[name] + k
+        return pltpu.make_async_remote_copy(
+            src_ref=src,
+            dst_ref=dst,
+            send_sem=self.send.at[i],
+            recv_sem=self.recv.at[i],
+            device_id=there,
+            device_id_type=MESH,
+        )
+
+    def start(self, name, k, ends, there, when=None):
+        at = k if callable(k) else lambda: k
+        self.copy(name, at(), *ends(), there).start()
+
+        def finish():
+            self.copy(name, at(), *ends(), there).wait_send()
+
+        self.late.append((finish, when))
+
+    def arrived(self, name, k, dst, there):
+        self.copy(name, k, dst, dst, there).wait_recv()
+
+    def finish(self):
+        for act, when in self.late:
+            if when is None:
+                act()
+            else:
+                pl.when(when())(act)
+
+
+def sides(me, rnd):
+    z = me.z
+    if rnd == 0:
+        return [(z, None, None)]
+    return [(z - rnd, True, lambda: z >= rnd), (z + rnd, False, lambda: z + rnd < NZ)]
+
+
+def line_round(me, lanes, name, rnd, ref_of, arrive):
+    z = me.z
+    left, right = me.at(z=z - 1), me.at(z=z + 1)
+
+    def go(zi, to_right, when):
+        def side():
+            return z < NZ - 1 if to_right else z > 0
+
+        def whole():
+            return side() if when is None else jnp.logical_and(when(), side())
+
+        lane, there = name + ("R" if to_right else "L"), right if to_right else left
+
+        def copy():
+            return lanes.copy(lane, zi, ref_of(zi), ref_of(zi), there)
+
+        pl.when(side())(lambda: copy().start())
+        lanes.late.append((lambda: copy().wait_send(), whole))
+
+    for zi, from_left, ok in sides(me, rnd):
+        if rnd == 0:
+            go(zi, True, None)
+            go(zi, False, None)
+            arrive(zi, None)
+            continue
+
+        @pl.when(ok())
+        def _(zi=zi, from_left=from_left, ok=ok):
+            lanes.arrived(name + ("R" if from_left else "L"), zi, ref_of(zi), left if from_left else right)
+            go(zi, from_left, ok)
+            arrive(zi, ok)
+
+
+def masked(i, j, blocks):
+    return j == i or j == 0 or i >= blocks - 2 or i - j >= WINDOW // B
+
+
+def keep(i, j, low, value, fill):
+    key_pos = lax.broadcasted_iota(jnp.int32, value.shape, 0) + j * B
+    ok = key_pos >= low
+    if i == j:
+        ok = ok & (key_pos <= lax.broadcasted_iota(jnp.int32, value.shape, 1) + i * B)
+    return jnp.where(ok, value, fill)
+
+
+def spans(i):
+    first = max(0, i - WINDOW // B)
+    return first, list(range(first, i + 1))
+
+
+def score_pass(i, h, slot, blocks, kn, qh, low_ref, S):
+    j0, js = spans(i)
+    cols = slice(i * B, (i + 1) * B)
+    qT = qh[h, 0:E, cols]
+    low = low_ref[0:1, cols]
+    top = jnp.full((1, B), FILL, f32)
+    for j in js:
+        s = nn(kn[h, j * B : (j + 1) * B, :], qT)
+        if masked(i, j, blocks):
+            s = keep(i, j, low, s, FILL)
+        S[slot, (j - j0) * B : (j - j0 + 1) * B, :] = s
+        top = jnp.maximum(top, jnp.max(s, axis=0, keepdims=True))
+    return top * (SCALE * LOG2E)
+
+
+def value_pass(i, h, slot, top, qh, S, o_ref, L_ref):
+    j0, js = spans(i)
+    total = jnp.zeros((1, B), f32)
+    out = jnp.zeros((E, B), f32)
+    for j in js:
+        p = jnp.exp2(S[slot, (j - j0) * B : (j - j0 + 1) * B, :] * (SCALE * LOG2E) - top)
+        total = total + jnp.sum(p, axis=0, keepdims=True)
+        out = out + nn(qh[h, 2 * E : 3 * E, j * B : (j + 1) * B], p.astype(bf))
+    half = i % 2
+    o_ref[i // 2, pl.ds(pl.multiple_of(h * E, E), E), half * B : (half + 1) * B] = (out / total).astype(bf)
+    L_ref[h, :, i * B : (i + 1) * B] = jnp.broadcast_to(top + jnp.log2(total), (8, B))
+
+
+def lows(seg, total):
+    pos = lax.broadcasted_iota(jnp.int32, (1, total), 1)
+    low = jnp.maximum(pos - (WINDOW - 1), 0)
+    first = seg[0:1, 0:1]
+    for d in range(1, 5):
+        begin = jnp.sum((seg < first + d).astype(f32), axis=1, keepdims=True).astype(jnp.int32)
+        low = jnp.where(seg >= first + d, jnp.maximum(low, begin), low)
+    return low
+
+
+def fwd_kernel(xo, w1, w2, cot, seg, n1, qh, o_ref, oin, L_ref, low_ref, W1T, W2g, cot2, wox, X4, W1, kn, S, send, recv):
+    me = Place()
+    dp, t, x, y, z, c = me.dp, me.t, me.x, me.y, me.z, me.c
+    total = n1.shape[0]
+    rows = xo.shape[0]
+    blocks = total // B
+    heads = kn.shape[0]
+    X_, Y_, C_, XC_ = me.at(x=1 - x), me.at(y=1 - y), me.at(c=1 - c), me.at(x=1 - x, c=1 - c)
+    lanes = Lanes(send, recv)
+    for name, count in (
+        ("aR", 4), ("aL", 4), ("ay", 4), ("x", 2), ("cx", 2), ("co", 1), ("cc", 1),
+        ("bR", 4), ("bL", 4), ("bx", 4), ("by", 4), ("bxy", 4), ("byx", 4), ("o", 4), ("w", 1),
+    ):
+        lanes.block(name, count)
+
+    me.greet(True)
+    W1[dp] = w1[...]
+    half = rows // 2
+
+    def a_ref(zi):
+        return W1.at[zi * 2 + y]
+
+    def a_arrive(zi, when):
+        lanes.start("ay", zi, lambda: (a_ref(zi), a_ref(zi)), Y_, when)
+
+    line_round(me, lanes, "a", 0, a_ref, a_arrive)
+    for k in range(2):
+        lanes.start("x", k, lambda k=k: (xo.at[pl.ds(k * half, half)], X4.at[t, pl.ds(k * half, half)]), X_)
+    lanes.start("co", 0, lambda: (xo, X4.at[t]), C_)
+    W2g[x, dp] = w2[...]
+    low_ref[...] = jnp.broadcast_to(lows(seg[...], total), low_ref.shape)
+    X4[t] = xo[...]
+    line_round(me, lanes, "a", 1, a_ref, a_arrive)
+    line_round(me, lanes, "a", 2, a_ref, a_arrive)
+    line_round(me, lanes, "a", 3, a_ref, a_arrive)
+
+    def b_ref(zi):
+        return W2g.at[x, zi * 2 + y]
+
+    def b_arrive(zi, when):
+        lanes.start("bx", zi, lambda: (b_ref(zi), b_ref(zi)), X_, when)
+        lanes.start("by", zi, lambda: (b_ref(zi), b_ref(zi)), Y_, when)
+
+    def b_corner(rnd):
+        def one(zi, ok):
+            def from_x():
+                return W2g.at[1 - x, zi * 2 + y]
+
+            def from_y():
+                return W2g.at[x, zi * 2 + 1 - y]
+
+            lanes.arrived("bx", zi, from_x(), X_)
+            lanes.start("bxy", zi, lambda: (from_x().at[:, 0:CUT],) * 2, Y_, ok)
+            lanes.arrived("by", zi, from_y(), Y_)
+            lanes.start("byx", zi, lambda: (from_y().at[:, CUT:],) * 2, X_, ok)
+
+        for zi, _, ok in sides(me, rnd):
+            if ok is None:
+                one(zi, None)
+            else:
+                pl.when(ok())(functools.partial(one, zi, ok))
+
+    def b_round(rnd):
+        line_round(me, lanes, "b", rnd, b_ref, b_arrive)
+
+    b_round(0)
+    for zi in range(NZ):
+        lanes.arrived("ay", zi, W1.at[zi * 2 + 1 - y], Y_)
+    W1T[...] = W1[...].reshape(W1.shape[0] * W1.shape[1], W1.shape[2]).T
+    lanes.start("cc", 0, lambda: (cot, cot2), C_)
+
+    def project(blk):
+        base = pl.multiple_of(blk * rows, rows)
+        gain = W1T[heads * 3 * E : heads * 3 * E + 16, :].astype(f32)[0:1]
+        value = X4[blk].astype(f32)
+        inv = lax.rsqrt(jnp.mean(value * value, axis=-1, keepdims=True) + 1e-05)
+        normed = (value * inv * gain).astype(bf)
+        n1[pl.ds(base, rows), :] = normed
+        out = nt(W1T[0 : heads * 3 * E, :], normed).astype(bf)
+        for h in range(heads):
+            qh[h, :, pl.ds(base, rows)] = out[h * 3 * E : (h + 1) * 3 * E]
+            kn[h, pl.ds(base, rows), :] = out[h * 3 * E + E : h * 3 * E + 2 * E].T
+
+    project(t)
+    lanes.arrived("co", 0, X4.at[x * 2 + 1 - c], C_)
+    project(x * 2 + 1 - c)
+    for k in range(2):
+        got = X4.at[(1 - x) * 2 + c, pl.ds(k * half, half)]
+        lanes.arrived("x", k, got, X_)
+        lanes.start("cx", k, lambda got=got: (got, got), C_)
+    project((1 - x) * 2 + c)
+    for k in range(2):
+        lanes.arrived("cx", k, X4.at[(1 - x) * 2 + 1 - c, pl.ds(k * half, half)], C_)
+    project((1 - x) * 2 + 1 - c)
+
+    b_round(1)
+
+    quarter_send = lanes.base["o"]
+
+    def quarter2(r):
+        def body(h, carry):
+            tops = []
+            for i in (2 * r, 2 * r + 1):
+                tops.append(score_pass(i, h, i % 2, blocks, kn, qh, low_ref, S))
+            for i in (2 * r, 2 * r + 1):
+                value_pass(i, h, i % 2, tops[i % 2], qh, S, o_ref, L_ref)
+            return carry
+
+        lax.fori_loop(0, heads, body, 0)
+
+        def out_copy():
+            return pltpu.make_async_remote_copy(
+                src_ref=o_ref.at[r],
+                dst_ref=oin.at[t],
+                send_sem=send.at[quarter_send + r],
+                recv_sem=recv.at[quarter_send + t],
+                device_id=(dp, r),
+                device_id_type=MESH,
+            )
+
+        @pl.when(t == r)
+        def _():
+            oin[t] = o_ref[r]
+
+        @pl.when(t != r)
+        def _():
+            out_copy().start()
+
+        lanes.late.append((lambda: out_copy().wait_send(), lambda: t != r))
+
+    quarter2(0)
+    b_corner(0)
+    b_round(2)
+    b_corner(1)
+    quarter2(1)
+    b_round(3)
+    quarter2(2)
+    b_corner(2)
+    quarter2(3)
+    b_corner(3)
+    for zi in range(NZ):
+        got = W2g.at[1 - x, zi * 2 + 1 - y]
+        lanes.arrived("bxy", zi, got.at[:, 0:CUT], Y_)
+        lanes.arrived("byx", zi, got.at[:, CUT:], X_)
+    wide = W2g.shape[3]
+    lanes.start("w", 0, lambda: (W2g.at[:, :, :, wide - 256 :], wox), C_)
+    lanes.arrived("cc", 0, cot2, C_)
+    for there in ((1 - x) * 2 + c, x * 2 + 1 - c, (1 - x) * 2 + 1 - c):
+        lanes.arrived("o", there, oin.at[there], (dp, there))
+    lanes.arrived("w", 0, wox, C_)
+    lanes.finish()
+
+
+N_SEM1 = 48
+VM = pl.BlockSpec(memory_space=pltpu.VMEM)
+
+
+def params(cid):
+    return pltpu.CompilerParams(collective_id=cid, has_side_effects=True, vmem_limit_bytes=60 * 2**20)
+
+
+def pack_weights(w_query, w_key, w_value, w_output, w_hidden, w_back, gain_one, gain_two):
+    part, width = w_query.shape
+    heads = width // E
+    joined = jnp.stack([w.reshape(part, heads, E) for w in (w_query, w_key, w_value)], axis=2).reshape(part, 3 * width)
+    gains = jnp.pad(jnp.stack([gain_one, gain_two], axis=1), ((0, 0), (0, 62)))
+    w1 = jnp.concatenate([joined, gains], axis=1)
+    w2 = jnp.concatenate([w_hidden, w_back.T, jnp.pad(w_output.T, ((0, 0), (0, 64)))], axis=1)
+    return w1, w2
+
+
+def run_fwd(xo, w1, w2, cot, seg):
+    rows, dm = xo.shape
+    total = seg.shape[1]
+    heads = 3
+    part = w1.shape[0]
+    s = jax.ShapeDtypeStruct
+    return pl.pallas_call(
+        fwd_kernel,
+        out_shape=(
+            s((total, dm), bf), s((heads, 3 * E, total), bf), s((4, heads * E, rows), bf), s((4, heads * E, rows), bf),
+            s((heads, 8, total), f32), s((8, total), jnp.int32), s((w1.shape[1], dm), bf),
+            s((2, 8, part, w2.shape[1]), bf), s((rows, dm), bf), s((2, 8, part, 256), bf),
+        ),
+        in_specs=[VM] * 5,
+        out_specs=(VM,) * 10,
+        scratch_shapes=[
+            pltpu.VMEM((4, rows, dm), bf),
+            pltpu.VMEM((8, part, w1.shape[1]), bf),
+            pltpu.VMEM((heads, total, E), bf),
+            pltpu.VMEM((2, WINDOW + B, B), f32),
+            pltpu.SemaphoreType.DMA((N_SEM1,)),
+            pltpu.SemaphoreType.DMA((N_SEM1,)),
+        ],
+        compiler_params=params(1),
+    )(xo, w1, w2, cot, seg)
+
+
+def gelu_and_slope(u):
+    root = 0.7978845608028654
+    square = u * u
+    th = jnp.tanh(u * (root + (root * 0.044715) * square))
+    half = 0.5 + 0.5 * th
+    slope = half + (0.5 * u) * (1.0 - th * th) * (root + (3.0 * root * 0.044715) * square)
+    return u * half, slope
+
+
+def norm_pull(value, gain, grad):
+    inv = lax.rsqrt(jnp.mean(value * value, axis=-1, keepdims=True) + 1e-05)
+    scaled = grad * gain
+    return inv * scaled - value * (inv * inv * inv * jnp.mean(value * scaled, axis=-1, keepdims=True))
+
+
+HB = 256
+
+
+def mid_kernel(xo, cot, cot2, oin, W2g, wox, W1T, G, do_ref, dx1, result,
+               wo, x1, n2b, cb, n2T, cT, res, dn2, sres, sdn, rres, rdn, dsend, gws, gwr, send, recv):
+    me = Place()
+    dp, t, x, c = me.dp, me.t, me.x, me.c
+    rows, dm = xo.shape
+    width = oin.shape[1]
+    C_ = me.at(c=1 - c)
+    lanes = Lanes(send, recv)
+    for name, count in (("n2", 1), ("dn", 1), ("rs", 1), ("gw", 1), ("do", 4)):
+        lanes.block(name, count)
+    me.greet(True)
+    wide = W2g.shape[2]
+    ff = (wide - 256) // 2
+    for xs in range(2):
+        wo[pl.ds(pl.multiple_of((xs * 2 + c) * width, width), width), :] = W2g[xs, :, 2 * ff : 2 * ff + width].T
+        wo[pl.ds(pl.multiple_of((xs * 2 + 1 - c) * width, width), width), :] = wox[xs, :, 0:width].T
+    gains = W1T[3 * width : 3 * width + 16, :].astype(f32)
+    gain = gains[1:2]
+    mid = xo[...].astype(f32) + tn(oin[...].reshape(4 * width, rows), wo[...])
+    x1[...] = mid
+    inv = lax.rsqrt(jnp.mean(mid * mid, axis=-1, keepdims=True) + 1e-05)
+    n2b[0:rows, :] = (mid * inv * gain).astype(bf)
+    lanes.start("n2", 0, lambda: (n2b.at[pl.ds(0, rows)], n2b.at[pl.ds(rows, rows)]), C_)
+    cb[0:rows, :] = cot[...]
+    cb[rows:, :] = cot2[...]
+    cT[...] = cb[...].T
+    res[...] = jnp.zeros_like(res)
+    dn2[...] = jnp.zeros_like(dn2)
+    n2T[:, 0:rows] = n2b[0:rows, :].T
+    lanes.arrived("n2", 0, n2b.at[pl.ds(rows, rows)], C_)
+    n2T[:, rows:] = n2b[rows:, :].T
+    per = ff // HB
+
+    def body(k, carry):
+        xs = lax.rem(x + lax.div(k, per), 2)
+        col = pl.multiple_of(lax.rem(k, per) * HB, HB)
+        wh = W2g[xs, :, pl.ds(col, HB)]
+        wb = W2g[xs, :, pl.ds(ff + col, HB)]
+        u = nn(n2b[...], wh)
+        act, slope = gelu_and_slope(u)
+        act = act.astype(bf)
+        du = (nn(cb[...], wb) * slope).astype(bf)
+        dn2[...] += nt(du, wh)
+        res[...] += nt(act, wb)
+        G[xs, :, pl.ds(col, HB)] = nn(n2T[...], du).astype(bf)
+        G[xs, :, pl.ds(ff + col, HB)] = nn(cT[...], act).astype(bf)
+        return carry
+
+    lax.fori_loop(0, 2 * per, body, 0)
+    sdn[...] = dn2[rows:, :].astype(bf)
+    lanes.start("dn", 0, lambda: (sdn, rdn), C_)
+    sres[...] = res[rows:, :].astype(bf)
+    lanes.start("rs", 0, lambda: (sres, rres), C_)
+    lanes.arrived("dn", 0, rdn, C_)
+    back = cot[...].astype(f32) + norm_pull(x1[...], gain, dn2[0:rows, :] + rdn[...].astype(f32))
+    dx1[...] = back
+    back = back.astype(bf)
+    out = nt(wo[...], back).astype(bf)
+    for r in range(4):
+        dsend[r] = out[r * width : (r + 1) * width]
+
+        def to_owner(r=r):
+            i = lanes.base["do"]
+            return pltpu.make_async_remote_copy(
+                src_ref=dsend.at[r], dst_ref=do_ref.at[t], send_sem=send.at[i + r], recv_sem=recv.at[i + t],
+                device_id=(dp, r), device_id_type=MESH,
+            )
+
+        @pl.when(t == r)
+        def _():
+            do_ref[t] = dsend[r]
+
+        pl.when(t != r)(lambda: to_owner().start())
+        lanes.late.append((lambda r=r, f=to_owner: f(r).wait_send(), lambda r=r: t != r))
+    gw = nt(back.T, oin[...].reshape(4 * width, rows)).astype(bf)
+    for xs in range(2):
+        even, odd = gw[:, 2 * xs * width : (2 * xs + 1) * width], gw[:, (2 * xs + 1) * width : (2 * xs + 2) * width]
+        G[xs, :, 2 * ff : 2 * ff + width] = jnp.where(c == 0, even, odd)
+        G[xs, :, 2 * ff + width :] = jnp.zeros((dm, wide - 2 * ff - width), bf)
+        gws[xs, :, 0:width] = jnp.where(c == 0, odd, even)
+        gws[xs, :, width:] = jnp.zeros((dm, 256 - width), bf)
+    lanes.start("gw", 0, lambda: (gws, gwr), C_)
+    lanes.arrived("rs", 0, rres, C_)
+    result[...] = (x1[...] + res[0:rows, :] + rres[...].astype(f32)).astype(bf)
+    lanes.arrived("gw", 0, gwr, C_)
+    for xs in range(2):
+        cols = slice(2 * ff, 2 * ff + width)
+        G[xs, :, cols] = (G[xs, :, cols].astype(f32) + gwr[xs, :, 0:width].astype(f32)).astype(bf)
+    for there in ((1 - x) * 2 + c, x * 2 + 1 - c, (1 - x) * 2 + 1 - c):
+        lanes.arrived("do", there, do_ref.at[there], (dp, there))
+    lanes.finish()
+
+
+def run_mid(xo, cot, cot2, oin, W2g, wox, W1T):
+    rows, dm = xo.shape
+    wide = W2g.shape[2]
+    width = oin.shape[1]
+    s = jax.ShapeDtypeStruct
+    v = pltpu.VMEM
+    return pl.pallas_call(
+        mid_kernel,
+        out_shape=(s((2, dm, wide), bf), s((4, width, rows), bf), s((rows, dm), f32), s((rows, dm), bf)),
+        in_specs=[VM] * 7,
+        out_specs=(VM,) * 4,
+        scratch_shapes=[
+            v((dm, dm), bf), v((rows, dm), f32), v((2 * rows, dm), bf), v((2 * rows, dm), bf),
+            v((dm, 2 * rows), bf), v((dm, 2 * rows), bf), v((2 * rows, dm), f32), v((2 * rows, dm), f32),
+            v((rows, dm), bf), v((rows, dm), bf), v((rows, dm), bf), v((rows, dm), bf),
+            v((4, width, rows), bf), v((2, dm, 256), bf), v((2, dm, 256), bf),
+            pltpu.SemaphoreType.DMA((8,)), pltpu.SemaphoreType.DMA((8,)),
+        ],
+        compiler_params=params(2),
+    )(xo, cot, cot2, oin, W2g, wox, W1T)
+
+
+def bwd_kernel(xo, dx1, n1, qh, o_ref, do_ref, L_ref, low_ref, W1T, G0, w1, w2,
+               gin, g1s, g2s, gains, G, dqh, kn, vn, dk, dv, X4, R1, R2, G1, RY, RZ, RA, RB, RA2, RB2, ZL, ZR, gs, gr, send, recv):
+    me = Place()
+    dp, t, x, y, z, c = me.dp, me.t, me.x, me.y, me.z, me.c
+    rows, dm = xo.shape
+    total = n1.shape[0]
+    blocks = total // B
+    heads = qh.shape[0]
+    part = w1.shape[0]
+    X_, Y_, C_, XC_ = me.at(x=1 - x), me.at(y=1 - y), me.at(c=1 - c), me.at(x=1 - x, c=1 - c)
+    left, right = me.at(z=z - 1), me.at(z=z + 1)
+    lanes = Lanes(send, recv)
+    for name, count in (
+        ("ra", 8), ("rb", 8), ("ra2", 4), ("rb2", 4), ("zR", 4), ("zL", 4),
+        ("d1", 2), ("d2", 1), ("y1", 4 * heads), ("z1", 3 * heads), ("g", 3),
+    ):
+        lanes.block(name, count)
+    me.greet(True)
+    G[...] = G0[...]
+
+    pairs = [sides(me, rnd) for rnd in range(NZ)]
+
+    def each(rnd, act):
+        for zi, from_left, ok in pairs[rnd]:
+            if ok is None:
+                act(zi, from_left, None)
+            else:
+                pl.when(ok())(functools.partial(act, zi, from_left, ok))
+
+    def first(zi, from_left, ok):
+        for k in range(2):
+            lanes.start("ra", lambda k=k: zi * 2 + k, lambda k=k: (G.at[k, zi * 2 + 1 - y, :, 0:CUT], RA.at[zi, k]), Y_, ok)
+            lanes.start("rb", lambda k=k: zi * 2 + k, lambda k=k: (G.at[1 - x, zi * 2 + k, :, CUT:], RB.at[zi, k]), X_, ok)
+
+    def add(xs, di, cols, *more):
+        value = G[xs, di, :, cols].astype(f32)
+        for m in more:
+            value = value + m.astype(f32)
+        G[xs, di, :, cols] = value.astype(bf)
+
+    def second(zi, from_left, ok):
+        A, Bc = slice(0, CUT), slice(CUT, None)
+        for k in range(2):
+            lanes.arrived("ra", zi * 2 + k, RA.at[zi, k], Y_)
+            lanes.arrived("rb", zi * 2 + k, RB.at[zi, k], X_)
+        add(1 - x, zi * 2 + y, A, RA[zi, 1 - x])
+        lanes.start("ra2", zi, lambda: (G.at[1 - x, zi * 2 + y, :, 0:CUT], RA2.at[zi]), X_, ok)
+        add(x, zi * 2 + 1 - y, Bc, RB[zi, 1 - y])
+        lanes.start("rb2", zi, lambda: (G.at[x, zi * 2 + 1 - y, :, CUT:], RB2.at[zi]), Y_, ok)
+        add(x, zi * 2 + y, A, RA[zi, x])
+        add(x, zi * 2 + y, Bc, RB[zi, y])
+
+    def third(zi, from_left, ok):
+        lanes.arrived("ra2", zi, RA2.at[zi], X_)
+        lanes.arrived("rb2", zi, RB2.at[zi], Y_)
+        add(x, zi * 2 + y, slice(0, CUT), RA2[zi])
+        add(x, zi * 2 + y, slice(CUT, None), RB2[zi])
+
+    def chain(zi, to_left, ok):
+        @pl.when(z < NZ - 1 if to_left else z > 0)
+        def _():
+            lane, buf, there = ("zL", ZR, right) if to_left else ("zR", ZL, left)
+            lanes.arrived(lane, zi, buf.at[zi], there)
+            add(x, zi * 2 + y, slice(None), buf[zi])
+
+        def ends():
+            return G.at[x, zi * 2 + y], (ZR if to_left else ZL).at[zi]
+
+        lanes.start("zL" if to_left else "zR", zi, ends, left if to_left else right, ok)
+
+    def last():
+        @pl.when(z < NZ - 1)
+        def _():
+            lanes.arrived("zL", z, ZR.at[z], right)
+            add(x, dp, slice(None), ZR[z])
+
+        @pl.when(z > 0)
+        def _():
+            lanes.arrived("zR", z, ZL.at[z], left)
+            add(x, dp, slice(None), ZL[z])
+
+        g2s[...] = G[x, dp].astype(f32)
+
+    for rnd in (3, 2, 1, 0):
+        each(rnd, first)
+
+    def one_y(h):
+        for zi in range(NZ):
+            lanes.start_at("y1", h * 4 + zi, G1.at[h, zi * 2 + 1 - y], RY.at[h, zi], Y_)
+
+    def one_z(h):
+        for step in range(NZ):
+            zi = lax.rem(z + step, NZ)
+            lanes.arrived("y1", h * 4 + zi, RY.at[h, zi], Y_)
+            G1[h, zi * 2 + y] = (G1[h, zi * 2 + y].astype(f32) + RY[h, zi].astype(f32)).astype(bf)
+            if step:
+                lanes.start_at("z1", h * 3 + step - 1, G1.at[h, zi * 2 + y], RZ.at[h, step - 1], me.at(z=zi))
+
+    def one_last(h):
+        value = G1[h, dp].astype(f32)
+        for step in range(1, NZ):
+            lanes.arrived("z1", h * 3 + step - 1, RZ.at[h, step - 1], me.at(z=lax.rem(z + NZ - step, NZ)))
+            value = value + RZ[h, step - 1].astype(f32)
+        g1s[:, h * 256 : (h + 1) * 256] = value
+        return value
+
+    def rows_first(r):
+        xr, cr = r // 2, r % 2
+        piece = dqh[:, :, r * rows : (r + 1) * rows].reshape(heads * 3 * E, rows)
+        X4[r] = tn(piece, W1T[0 : heads * 3 * E, :]).astype(bf)
+        pl.when(c != cr)(lambda: lanes.start_at("d1", xr, X4.at[r], R1.at[xr], C_))
+
+    def rows_second(r):
+        xr, cr = r // 2, r % 2
+
+        @pl.when(c == cr)
+        def _():
+            lanes.arrived("d1", xr, R1.at[xr], C_)
+            X4[r] = (X4[r].astype(f32) + R1[xr].astype(f32)).astype(bf)
+            pl.when(x != xr)(lambda: lanes.start_at("d2", 0, X4.at[r], R2, X_))
+
+    events = {
+        (0, 7): [lambda: each(3, second)],
+        (0, 6): [lambda: each(2, second)],
+        (0, 5): [lambda: each(3, third), lambda: each(3, chain)],
+        (0, 3): [lambda: each(1, second)],
+        (0, 0): [lambda: each(2, third), lambda: each(2, chain)],
+        (1, 6): [lambda: each(0, second)],
+        (1, 4): [lambda: each(1, third), lambda: each(1, chain)],
+        (1, 2): [lambda: each(0, third)],
+    }
+
+    def head(h, carry):
+        kn[...] = qh[h, E : 2 * E, :].T
+        vn[...] = qh[h, 2 * E : 3 * E, :].T
+        for i in range(blocks)[::-1]:
+            j0, js = spans(i)
+            cols = slice(i * B, (i + 1) * B)
+            half = slice((i % 2) * B, (i % 2 + 1) * B)
+            hs = pl.ds(pl.multiple_of(h * E, E), E)
+            qT, doT = qh[h, 0:E, cols], do_ref[i // 2, hs, half]
+            low, L = low_ref[0:1, cols], L_ref[h, 0:1, cols]
+            D = jnp.sum(doT.astype(f32) * o_ref[i // 2, hs, half].astype(f32), axis=0, keepdims=True)
+            dq = jnp.zeros((E, B), f32)
+
+            def front(j):
+                ks = slice(j * B, (j + 1) * B)
+                return nn(kn[ks, :], qT), nn(vn[ks, :], doT)
+
+            queue = [front(j) for j in js[:2]]
+            for n, j in enumerate(js):
+                ks = slice(j * B, (j + 1) * B)
+                if n + 2 < len(js):
+                    queue.append(front(js[n + 2]))
+                s, dp_ = queue.pop(0)
+                p = jnp.exp2(s * (SCALE * LOG2E) - L)
+                if masked(i, j, blocks):
+                    p = keep(i, j, low, p, 0.0)
+                ds = (p * (dp_ - D)).astype(bf)
+                dvj, dkj = nt(doT, p.astype(bf)), nt(qT, ds)
+                if i == min(blocks - 1, j + WINDOW // B):
+                    dv[:, ks] = dvj
+                    dk[:, ks] = dkj
+                else:
+                    dv[:, ks] += dvj
+                    dk[:, ks] += dkj
+                dq = dq + nn(qh[h, E : 2 * E, ks], ds)
+            dqh[h, 0:E, cols] = (dq * SCALE).astype(bf)
+            dqh[h, E : 2 * E, cols] = (dk[:, cols] * SCALE).astype(bf)
+            dqh[h, 2 * E : 3 * E, cols] = dv[:, cols].astype(bf)
+            for k in range(heads):
+                for act in events.get((k, i), ()):
+                    pl.when(h == k)(act)
+            if i == 4:
+                pl.when(h > 0)(lambda: one_z(h - 1))
+            if i % 2 == 0:
+
+                @pl.when(h == heads - 1)
+                def _():
+                    rows_first(i // 2)
+                    if i // 2 < 3:
+                        rows_second(i // 2 + 1)
+
+        g = nn(dqh[h], n1[...]).T.astype(bf).reshape(8, part, 3 * E)
+        G1[h, :, :, 0 : 3 * E] = g
+        G1[h, :, :, 3 * E :] = jnp.zeros((8, part, 256 - 3 * E), bf)
+        one_y(h)
+        return carry
+
+    lax.fori_loop(0, heads, head, 0)
+    rows_second(0)
+    one_z(heads - 1)
+    last()
+    w1v, w2v = w1[...].astype(f32), w2[...].astype(f32)
+    sums = [one_last(h) for h in range(heads)]
+    gain1 = sum(
+        jnp.sum(sums[h][:, 0 : 3 * E] * w1v[:, h * 3 * E : (h + 1) * 3 * E], axis=1, keepdims=True) for h in range(heads)
+    ) / w1v[:, heads * 3 * E : heads * 3 * E + 1]
+    ff = (w2.shape[1] - 256) // 2
+    gain2 = jnp.sum(g2s[:, 0:ff] * w2v[:, 0:ff], axis=1, keepdims=True) / w1v[:, heads * 3 * E + 1 : heads * 3 * E + 2]
+    both_ = jnp.concatenate([gain1, gain2, jnp.zeros((part, 126), f32)], axis=1)
+    both_ = jnp.concatenate([both_, jnp.zeros((128 - part, 128), f32)], axis=0).T[0:8]
+    gs[...] = both_
+    for k, there in enumerate((X_, C_, XC_)):
+        lanes.start("g", k, lambda k=k: (gs, gr.at[k]), there)
+    gain = W1T[heads * 3 * E : heads * 3 * E + 16, :].astype(f32)[0:1]
+    lanes.arrived("d2", 0, R2, X_)
+    dn1 = X4[t].astype(f32) + R2[...].astype(f32)
+    gin[...] = (dx1[...] + norm_pull(xo[...].astype(f32), gain, dn1)).astype(bf)
+    for k, there in enumerate((X_, C_, XC_)):
+        lanes.arrived("g", k, gr.at[k], there)
+    gains[...] = gs[...] + gr[0] + gr[1] + gr[2]
+    for h in range(heads):
+        for zi in range(NZ):
+            lanes.copy("y1", h * 4 + zi, G1.at[h, zi * 2 + 1 - y], RY.at[h, zi], Y_).wait_send()
+        for step in range(1, NZ):
+            zi = lax.rem(z + step, NZ)
+            lanes.copy("z1", h * 3 + step - 1, G1.at[h, zi * 2 + y], RZ.at[h, step - 1], me.at(z=zi)).wait_send()
+    for r in range(4):
+        xr, cr = r // 2, r % 2
+        pl.when(c != cr)(lambda: lanes.copy("d1", xr, X4.at[r], R1.at[xr], C_).wait_send())
+        pl.when(jnp.logical_and(c == cr, x != xr))(lambda: lanes.copy("d2", 0, X4.at[r], R2, X_).wait_send())
+    lanes.finish()
+
+
+def start_at(self, name, k, src, dst, there):
+    self.copy(name, k, src, dst, there).start()
+
+
+Lanes.start_at = start_at
+
+
+def run_bwd(xo, dx1, n1, qh, o, do, L, low, W1T, G, w1, w2):
+    rows, dm = xo.shape
+    total = n1.shape[0]
+    heads = qh.shape[0]
+    part, wide = w2.shape
+    s, v = jax.ShapeDtypeStruct, pltpu.VMEM
+    return pl.pallas_call(
+        bwd_kernel,
+        out_shape=(s((rows, dm), bf), s((part, heads * 256), f32), s((part, wide), f32), s((8, 128), f32)),
+        in_specs=[VM] * 12,
+        out_specs=(VM,) * 4,
+        scratch_shapes=[
+            v(G.shape, bf), v(qh.shape, bf), v((total, E), bf), v((total, E), bf), v((E, total), f32), v((E, total), f32),
+            v((4, rows, dm), bf), v((2, rows, dm), bf), v((rows, dm), bf),
+            v((heads, 8, part, 256), bf), v((heads, 4, part, 256), bf), v((heads, 3, part, 256), bf),
+            v((4, 2, part, CUT), bf), v((4, 2, part, wide - CUT), bf), v((4, part, CUT), bf), v((4, part, wide - CUT), bf),
+            v((4, part, wide), bf), v((4, part, wide), bf), v((8, 128), f32), v((3, 8, 128), f32),
+            pltpu.SemaphoreType.DMA((64,)), pltpu.SemaphoreType.DMA((64,)),
+        ],
+        compiler_params=params(3),
+    )(xo, dx1, n1, qh, o, do, L, low, W1T, G, w1, w2)
+
+
+def block(inputs, segments, w_query, w_key, w_value, w_output, w_hidden, w_back, gain_one, gain_two, cotangent):
+    w1, w2 = pack_weights(w_query, w_key, w_value, w_output, w_hidden, w_back, gain_one, gain_two)
+    n1, qh, o, oin, L, low, W1T, W2g, cot2, wox = run_fwd(inputs, w1, w2, cotangent, segments.reshape(1, -1))
+    part, wide = w2.shape
+    dm = inputs.shape[1]
+    G, do, dx1, result = run_mid(inputs, cotangent, cot2, oin, W2g.reshape(2, dm, wide), wox.reshape(2, dm, 256), W1T)
+    gin, g1s, g2s, gains = run_bwd(inputs, dx1, n1, qh, o, do, L, low, W1T, G.reshape(2, 8, part, wide), w1, w2)
+    width = w_query.shape[1]
+    heads = width // E
+    ff = w_hidden.shape[1]
+    g1s = g1s.reshape(part, heads, 256)[:, :, : 3 * E].reshape(part, heads, 3, E)
+    gq, gk, gv = (g1s[:, :, k].reshape(part, width) for k in range(3))
+    mine = lax.dynamic_slice_in_dim(gains, lax.axis_index("tensor") * (part // 4), part // 4, axis=1)
+    return (result, gin, gq, gk, gv, g2s[:, 2 * ff : 2 * ff + width].T, g2s[:, :ff], g2s[:, ff : 2 * ff].T, mine[0], mine[1])
 
 
 def normed(value, gain):
@@ -229,29 +1016,10 @@
 
 
 def solution(mesh):
-    in_specs = (
-        P(("dp", "tensor"), None),
-        P("dp"),
-        P("dp", "tensor"),
-        P("dp", "tensor"),
-        P("dp", "tensor"),
-        P("tensor", "dp"),
-        P("dp", "tensor"),
-        P("tensor", "dp"),
-        P("dp"),
-        P("dp"),
-        P(("dp", "tensor"), None),
-    )
-    out_specs = (
-        P(("dp", "tensor"), None),
-        P(("dp", "tensor"), None),
-        P("dp", "tensor"),
-        P("dp", "tensor"),
-        P("dp", "tensor"),
-        P("tensor", "dp"),
-        P("dp", "tensor"),
-        P("tensor", "dp"),
-        P(("dp", "tensor")),
-        P(("dp", "tensor")),
-    )
-    return jax.shard_map(shards, mesh=mesh, in_specs=in_specs, out_specs=out_specs, check_vma=False)
+    rows, cols = P(("dp", "tensor"), None), P("dp", "tensor")
+    turned, part = P("tensor", "dp"), P("dp")
+    in_specs = (rows, part, cols, cols, cols, turned, cols, turned, part, part, rows)
+    out_specs = (rows, rows, cols, cols, cols, turned, cols, turned, P(("dp", "tensor")), P(("dp", "tensor")))
+    here = mesh.shape["dp"] == 2 * NZ and mesh.shape["tensor"] == 4
+    body = block if here else shards
+    return jax.shard_map(body, mesh=mesh, in_specs=in_specs, out_specs=out_specs, check_vma=False)

time: 1020 us -> 253 us (0.25)
  waiting for transfers between devices: 430 us -> 0 us
  Pallas kernels: 0 us -> 231 us
  matrix products: 220 us -> 0 us
  blocking collectives: 188 us -> 0 us
  other arithmetic: 94.8 us -> 3.2 us
  loops' own time: 26.4 us -> 0 us
  local copies, waits for them, and re-layouts: 34.6 us -> 13.4 us
  between operations: 15.7 us -> 0.75 us
    pallas_call x0 -> x3, Pallas kernels: none -> 231 us  [the longest x1 105 us: run_bwd(): pl.pallas_call(bwd_kernel, out_shape=(s((rows, dm), bf), s((part, heads *...]
    dot_general x39 -> x0, matrix products: 216 us -> none  [the longest x8 35.9 us: scores_for(): jnp.einsum('qhe,khe->hqk', query_block, key_rows, preferred_element_type=...]
    unnamed x20 -> x0, waiting for transfers between devices: 198 us -> none
    reduce_scatter x5 -> x0, waiting for transfers between devices: 177 us -> none  [the longest x1 72.3 us: shards(): lax.psum_scatter(grad_w_back, 'dp', scatter_dimension=1, tiled=True)]
    all_gather x4 -> x0, blocking collectives: 125 us -> none  [the longest x1 31.9 us: shards(): lax.all_gather(owned[1], 'dp', axis=0, tiled=True)]
    unnamed x2 -> x0, blocking collectives: 63 us -> none
    all_gather x7 -> x0, waiting for transfers between devices: 43.3 us -> none  [the longest x1 25.8 us: shards(): lax.all_gather(grad_middle.astype(jnp.bfloat16), 'tensor', axis=0, tiled=...]
    convert_element_type x10 -> x0, other arithmetic: 34.6 us -> none  [the longest x4 24.5 us: backward_block(): grad_scores = (probability * (grad_probs - delta_rows)).astype(jnp.bfloat16)]
  transfers between devices with their start and end apart: 17 -> 0, of which waited for: 9 -> 0; matrix products, arithmetic and copies ran while one was open for 30% -> 0% of each run, Pallas kernels for 0% -> 0%
where the time goes in v1:
time: 253 us; the launch traced here: 248 us
  Pallas kernels  231 us (91%)
  local copies, waits for them, and re-layouts  13.4 us (5%)
  other arithmetic  3.2 us (1%)
    pallas_call x1, Pallas kernels, run_bwd(): pl.pallas_call(bwd_kernel, out_shape=(s((rows, dm), bf), s((part, heads *...  105 us
    pallas_call x1, Pallas kernels, run_fwd(): pl.pallas_call(fwd_kernel, out_shape=(s((total, dm), bf), s((heads, 3 * E...  83.3 us
    pallas_call x1, Pallas kernels, run_mid(): pl.pallas_call(mid_kernel, out_shape=(s((2, dm, wide), bf), s((4, width,...  43.1 us
    unnamed x16, local copies, waits for them, and re-layouts  8.32 us

profile of v1, /device:TPU:0, one launch (start us, length us, event | category | flops | bytes accessed | tf_op | source)
XLA Modules:
  0.0 248.4 jit_solution(3874622325271313690)
XLA Ops:
  0.6 0.9 copy.44
  1.5 0.9 copy.45
  2.5 0.9 copy.46
  3.5 0.1 copy.49
  3.6 0.7 pad_maximum_fusion.1
  4.3 0.1 copy.48
  4.4 0.7 fusion.3.w1
  5.2 0.9 copy.50
  6.0 1.7 fusion.1.w2
  7.8 83.3 %shard_map.186 = (bf16[2048,768]{1,0:T(8,128)(2,1)}, bf16[3,192,2048]{2,1,0:T(8,128)(2,1)}, bf16[4,192,512]{2,1,0:T(8,128)(2,1)}, bf16[4,192,512]{2,1,0:T(8,128)...) custom-call(bf16[512,768]{1,0:T(8,128)(2,1)} %xo.5, ...), custom_call_target="tpu_custom_call" | custom-call | tf_op jit(solution)/shard_map/pallas_call | solution.py:372
  91.1 43.1 %shard_map.187 = (bf16[2,768,1792]{2,1,0:T(8,128)(2,1)}, bf16[4,192,512]{2,1,0:T(8,128)(2,1)}, f32[512,768]{1,0:T(8,128)}, bf16[512,768]{1,0:T(8,128)(2,1)}) custom-call(bf16[512,768]{1,0:T(8,128)(2,1)} %xo.5, bf16[512,768]{1,0:T(8,128)(2,1)} %cot.3, bf16[512,768]{1,0:T(8,128)(2,1)} %get-tuple-element.28.cot2, bf16[4,192,512]{2,1,0:T(8,128)(2,1)} %get-tuple-element.29.oin, ...), custom_call_target="tpu_custom_call" | custom-call | tf_op jit(solution)/shard_map/pallas_call | solution.py:510
  134.2 104.6 %shard_map.188 = (bf16[512,768]{1,0:T(8,128)(2,1)}, f32[96,768]{1,0:T(8,128)}, f32[96,1792]{1,0:T(8,128)}, f32[8,128]{1,0:T(8,128)}) custom-call(bf16[512,768]{1,0:T(8,128)(2,1)} %xo.5, f32[512,768]{1,0:T(8,128)} %get-tuple-element.34.dx1, bf16[2048,768]{1,0:T(8,128)(2,1)} %get-tuple-element.35.n1, bf16[3,192,2048]{2,1,0:T(8,128)(2,1)} %get-tuple-element.36.qh, ...), custom_call_target="tpu_custom_call" | custom-call | tf_op jit(solution)/shard_map/pallas_call | solution.py:764
  238.8 0.0 copy-start.2
  238.8 0.0 copy-start
  238.8 0.0 copy-start.1
  238.8 1.2 reshape.46
  240.1 0.2 copy.51
  240.3 0.7 copy.52
  241.0 0.7 copy.53
  241.7 0.7 copy.54
  242.5 1.9 slice_bitcast_fusion
  244.4 0.9 slice_bitcast_fusion.1
  245.3 0.7 copy.55
  246.0 0.0 copy-done.2
  246.0 0.1 constant_dynamic-slice_fusion
  246.1 0.5 slice_bitcast_fusion.2
  246.6 0.0 copy-done
  246.6 0.9 copy.58
  247.5 0.0 copy-done.1
  247.5 0.9 copy.59
  (3 shorter events, 0.1 us)
Async XLA Ops:
  238.8 7.2 %copy-start.2 = (f32[8,128]{1,0:T(8,128)S(1)}, f32[8,128]{1,0:T(8,128)}, u32[]{:S(2)}) copy-start(f32[8,128]{1,0:T(8,128)} %get-tuple-element.45) | copy-start | bytes 12292
  238.8 7.8 %copy-start = (bf16[512,768]{1,0:T(8,128)(2,1)S(1)}, bf16[512,768]{1,0:T(8,128)(2,1)}, u32[]{:S(2)}) copy-start(bf16[512,768]{1,0:T(8,128)(2,1)} %get-tuple-element.93) | copy-start | bytes 2359300
  238.8 8.7 %copy-start.1 = (bf16[512,768]{1,0:T(8,128)(2,1)S(1)}, bf16[512,768]{1,0:T(8,128)(2,1)}, u32[]{:S(2)}) copy-start(bf16[512,768]{1,0:T(8,128)(2,1)} %get-tuple-element.94) | copy-start | bytes 2359300
